TPU v7x, 128 devices: a whole 4x4x4 slice. The times are simulated.
128 devices in a mesh: grp: 8 (over y, core), ingrp: 16 (over x, z).
Axes of the slice: x: 4, y: 4, z: 4, core: 2. Of those that a mesh axis runs over, the one named last changes fastest.
Arguments:
- tokens: bfloat16 [16384, 3584], P(('grp', 'ingrp')), may hold values from -6 to 6
- out_grad: bfloat16 [16384, 3584], P(('grp', 'ingrp')), may hold values from -1.5 to 1.5
- route_weights: bfloat16 [16384, 4], P(('grp', 'ingrp')), may hold values from 0.049804688 to 0.59765625
- expert_ids: int32 [16384, 4], P(('grp', 'ingrp')), may hold values from 0 to 127, as said below
- w_gate: bfloat16 [128, 3584, 1024], P(('grp', 'ingrp')), may hold values from -0.09375 to 0.09375
- w_up: bfloat16 [128, 3584, 1024], P(('grp', 'ingrp')), may hold values from -0.09375 to 0.09375
- w_down: bfloat16 [128, 1024, 3584], P(('grp', 'ingrp')), may hold values from -0.1875 to 0.1875
Outputs:
- x_grad: bfloat16 [16384, 3584], P(('grp', 'ingrp'))
- route_grad: float32 [16384, 4], P(('grp', 'ingrp'))
Inputs may be any that keep to these rules, and one draw needn't show every extreme that they name: `expert_ids`: each token names 4 distinct experts in 2 distinct node groups, 2 in each; expert e lies in group e // 16, and ids k and k + 1 with k even lie in one group. Of each device's tokens every group is chosen by exactly 32, and at most 8 name any one expert; in every draw one and the same expert of each group is named by exactly 8 tokens of every device, so that expert receives 1024 rows in all.
All inputs are finite; a program needn't handle non-finite values.
Results may differ from a plain program's by a relative error of at most 0.0049.
Values may be sent and summed in bfloat16 or wider, within the bound.
No kernel may reach another device: no remote copies, remote signals or barrier semaphores. Data moves between devices by JAX's collectives and lax.ppermute only.
A program may use at most 128 MiB of HBM per device.

v0:
```python
import jax
import jax.numpy as jnp
from jax import lax
from jax.sharding import PartitionSpec as P

TILE = 128


def expert_rows(rows_x, rows_dy, rows_w, gate_mat, up_mat, down_mat):
    gate = jnp.dot(rows_x, gate_mat, preferred_element_type=jnp.float32)
    upper = jnp.dot(rows_x, up_mat, preferred_element_type=jnp.float32)
    sigma = jax.nn.sigmoid(gate)
    active = gate * sigma
    hidden = active * upper
    raw_grad = lax.dot_general(
        rows_dy, down_mat, (((1,), (1,)), ((), ())), preferred_element_type=jnp.float32
    )
    route_part = jnp.sum(raw_grad * hidden, axis=1)
    hidden_grad = rows_w[:, None] * raw_grad
    d_gate = (hidden_grad * upper * sigma * (1.0 + gate * (1.0 - sigma))).astype(jnp.bfloat16)
    d_upper = (hidden_grad * active).astype(jnp.bfloat16)
    contrib = lax.dot_general(
        d_gate, gate_mat, (((1,), (1,)), ((), ())), preferred_element_type=jnp.float32
    )
    contrib = contrib + lax.dot_general(
        d_upper, up_mat, (((1,), (1,)), ((), ())), preferred_element_type=jnp.float32
    )
    return (contrib, route_part)


def expert_block(rows_x, rows_dy, rows_w, gate_mat, up_mat, down_mat):
    row_count, width = rows_x.shape
    live = (rows_w != 0).astype(jnp.int32)
    position = jnp.cumsum(live) - 1
    live_total = jnp.sum(live)
    padded_rows = (row_count + TILE - 1) // TILE * TILE
    packed = (
        jnp.full((padded_rows,), row_count, jnp.int32)
        .at[jnp.where(live > 0, position, padded_rows)]
        .set(jnp.arange(row_count, dtype=jnp.int32), mode="drop")
    )
    x_padded = jnp.concatenate([rows_x, jnp.zeros((1, width), rows_x.dtype)], axis=0)
    dy_padded = jnp.concatenate([rows_dy, jnp.zeros((1, width), rows_dy.dtype)], axis=0)
    w_padded = jnp.concatenate([rows_w, jnp.zeros((1,), rows_w.dtype)], axis=0)
    tile_count = (live_total + TILE - 1) // TILE

    def one_tile(tile_step, carry):
        grads, routes = carry
        picked = lax.dynamic_slice_in_dim(packed, tile_step * TILE, TILE)
        contrib, route_part = expert_rows(
            x_padded[picked],
            dy_padded[picked],
            w_padded[picked].astype(jnp.float32),
            gate_mat,
            up_mat,
            down_mat,
        )
        return (grads.at[picked].set(contrib), routes.at[picked].set(route_part))

    start = (
        jnp.zeros((row_count + 1, width), jnp.float32),
        jnp.zeros((row_count + 1,), jnp.float32),
    )
    grads, routes = lax.fori_loop(0, tile_count, one_tile, start)
    return (grads[:row_count], routes[:row_count])


def ranks_of(labels, label_count):
    onehot = (labels[:, None] == jnp.arange(label_count, dtype=jnp.int32)[None, :]).astype(
        jnp.int32
    )
    return jnp.sum((jnp.cumsum(onehot, axis=0) - onehot) * onehot, axis=1)


def local(tokens, out_grad, route_weights, expert_ids, w_gate, w_up, w_down):
    tok_rows, width = tokens.shape
    top_count = expert_ids.shape[1]
    groups_count = lax.axis_size("grp")
    members = lax.axis_size("ingrp")
    experts = groups_count * members
    capacity = 2 * tok_rows * top_count // experts
    gate_mat = w_gate[0]
    up_mat = w_up[0]
    down_mat = w_down[0]
    x_padded = jnp.concatenate([tokens, jnp.zeros((1, width), tokens.dtype)], axis=0)
    dy_padded = jnp.concatenate([out_grad, jnp.zeros((1, width), out_grad.dtype)], axis=0)
    pair_total = tok_rows * top_count
    pair_ids = expert_ids.reshape(-1)
    slots = pair_ids * capacity + ranks_of(pair_ids, experts)
    sources = (
        jnp.full((experts * capacity,), pair_total, jnp.int32)
        .at[slots]
        .set(jnp.arange(pair_total, dtype=jnp.int32))
    )
    owners = sources // top_count
    weight_padded = jnp.concatenate(
        [route_weights.reshape(-1), jnp.zeros((1,), route_weights.dtype)]
    )
    grid_shape = (groups_count, members, capacity, width)
    sent = (
        x_padded[owners].reshape(grid_shape),
        dy_padded[owners].reshape(grid_shape),
        weight_padded[sources].reshape(grid_shape[:3]),
    )
    arrived = (
        lax.all_to_all(
            lax.all_to_all(sent[0], "grp", split_axis=0, concat_axis=0, tiled=True),
            "ingrp",
            split_axis=1,
            concat_axis=1,
            tiled=True,
        ),
        lax.all_to_all(
            lax.all_to_all(sent[1], "grp", split_axis=0, concat_axis=0, tiled=True),
            "ingrp",
            split_axis=1,
            concat_axis=1,
            tiled=True,
        ),
        lax.all_to_all(
            lax.all_to_all(sent[2], "grp", split_axis=0, concat_axis=0, tiled=True),
            "ingrp",
            split_axis=1,
            concat_axis=1,
            tiled=True,
        ),
    )
    row_total = experts * capacity
    grads, routes = expert_block(
        arrived[0].reshape(row_total, width),
        arrived[1].reshape(row_total, width),
        arrived[2].reshape(row_total),
        gate_mat,
        up_mat,
        down_mat,
    )
    back = (
        lax.all_to_all(
            lax.all_to_all(
                grads.reshape(grid_shape), "grp", split_axis=0, concat_axis=0, tiled=True
            ),
            "ingrp",
            split_axis=1,
            concat_axis=1,
            tiled=True,
        ),
        lax.all_to_all(
            lax.all_to_all(
                routes.reshape(grid_shape[:3]), "grp", split_axis=0, concat_axis=0, tiled=True
            ),
            "ingrp",
            split_axis=1,
            concat_axis=1,
            tiled=True,
        ),
    )
    back_grads = back[0].reshape(row_total, width)
    back_routes = back[1].reshape(row_total)
    x_grad = jnp.sum(back_grads[slots].reshape(tok_rows, top_count, width), axis=1).astype(
        jnp.bfloat16
    )
    route_grad = back_routes[slots].reshape(tok_rows, top_count)
    return (x_grad, route_grad)


def solution(mesh):
    return jax.shard_map(
        local,
        mesh=mesh,
        in_specs=(
            P(("grp", "ingrp"), None),
            P(("grp", "ingrp"), None),
            P(("grp", "ingrp"), None),
            P(("grp", "ingrp"), None),
            P(("grp", "ingrp"), None, None),
            P(("grp", "ingrp"), None, None),
            P(("grp", "ingrp"), None, None),
        ),
        out_specs=(P(("grp", "ingrp"), None), P(("grp", "ingrp"), None)),
        check_vma=False,
    )
```

profile of v0, /device:TPU:6, one launch (start us, length us, event | category | flops | bytes accessed | tf_op | source)
XLA Modules:
  0.0 1378.4 jit_solution(7182607052093267069)
XLA Ops:
  3.2 2.4 scatter_custom_fusion.2
  6.7 6.8 gather_fusion.3
  13.7 9.6 all_to_all.50
  24.0 8.3 all-to-all-start.1
  33.5 7.3 gather_fusion.4
  40.8 5.0 all-to-all-start.2
  45.9 7.3 gather_fusion.5
  53.2 76.0 %all-to-all-done.2 = bf16[8,16,8,3584]{3,2,1,0:T(8,128)(2,1)} async-done(((bf16[8,16,8,3584]{3,2,1,0:T(8,128)(2,1)}), bf16[8,16,8,3584]{3,2,1,0:T(8,128)(2,1)}, u32[]{:S(2)}, u32[]{:S(2)}) %all-to-all-start.2) | async-done | bytes 7340064 | tf_op jit(solution)/shard_map/all_to_all | solution.py:114
  129.2 4.8 all-to-all-start.4
  134.0 6.8 copy.88
  140.9 76.5 %all-to-all-done.4 = bf16[8,16,8,3584]{3,2,1,0:T(8,128)(2,1)} async-done(((bf16[8,16,8,3584]{3,2,1,0:T(8,128)(2,1)}), bf16[8,16,8,3584]{3,2,1,0:T(8,128)(2,1)}, u32[]{:S(2)}, u32[]{:S(2)}) %all-to-all-start.4) | async-done | bytes 7340064 | tf_op jit(solution)/shard_map/all_to_all | solution.py:107
  217.4 7.2 all-to-all-start.3
  224.6 6.8 copy.90
  231.5 116.7 %all-to-all-done.3 = bf16[8,16,8,3584]{3,2,0,1:T(8,128)(2,1)} async-done(((bf16[8,16,8,3584]{3,2,0,1:T(8,128)(2,1)}), bf16[8,16,8,3584]{3,2,0,1:T(8,128)(2,1)}, u32[]{:S(2)}, u32[]{:S(2)}) %all-to-all-start.3) | async-done | bytes 7340064 | tf_op jit(solution)/shard_map/all_to_all | solution.py:113
  348.1 9.4 all-to-all-start.5
  360.2 4.3 scatter_custom_fusion.3
  364.5 3.8 copy.89
  368.3 3.4 concatenate.21
  371.7 77.4 %all-to-all-done.5 = bf16[8,16,8,3584]{3,2,0,1:T(8,128)(2,1)} async-done(((bf16[8,16,8,3584]{3,2,0,1:T(8,128)(2,1)}), bf16[8,16,8,3584]{3,2,0,1:T(8,128)(2,1)}, u32[]{:S(2)}, u32[]{:S(2)}) %all-to-all-start.5) | async-done | bytes 7340064 | tf_op jit(solution)/shard_map/all_to_all | solution.py:106
  449.1 3.8 copy.91
  452.9 3.4 concatenate.23
  456.3 7.1 broadcast_in_dim.14
  463.4 210.5 %while.12 = (s32[]{:T(128)}, f32[1025,3584]{1,0:T(8,128)}, f32[1025]{0:T(1024)S(1)}, s32[]{:T(128)}, s32[1024]{0:T(1024)S(1)}, /*index=5*/bf16[1025]{0:T(1024)(1...) while((s32[]{:T(128)}, f32[1025,3584]{1,0:T(8,128)}, ...), condition=%wide.region_12.13_spmd, body=%wide.region_8.12_spmd.sunk | while | flops 4701357568 | bytes 88748504 | solution.py:64
  473.3 6.1 gather_fusion
  479.4 4.5 fusion.51
  485.8 6.1 gather_fusion.1
  491.9 5.7 multiply_reduce_fusion.2
  498.9 5.7 fusion.53
  504.6 5.7 convolution_add_fusion.2
  510.3 12.0 scatter_fusion
  523.5 6.1 gather_fusion
  529.5 4.5 fusion.51
  536.0 6.1 gather_fusion.1
  542.0 5.7 multiply_reduce_fusion.2
  549.0 5.7 fusion.53
  554.7 5.7 convolution_add_fusion.2
  560.5 12.0 scatter_fusion
  573.6 6.1 gather_fusion
  579.7 4.5 fusion.51
  586.1 6.1 gather_fusion.1
  592.2 5.7 multiply_reduce_fusion.2
  599.1 5.7 fusion.53
  604.9 5.7 convolution_add_fusion.2
  610.6 12.0 scatter_fusion
  623.7 6.1 gather_fusion
  629.8 4.5 fusion.51
  636.2 6.1 gather_fusion.1
  642.3 5.7 multiply_reduce_fusion.2
  649.2 5.7 fusion.53
  655.0 5.7 convolution_add_fusion.2
  660.7 12.0 scatter_fusion
  674.7 12.9 all-to-all-start.8
  687.6 11.3 slice.23
  698.9 5.5 all-to-all-start.6
  706.5 160.1 %all-to-all-done.6 = f32[8,16,8,3584]{3,2,1,0:T(8,128)} async-done(((f32[8,16,8,3584]{3,2,1,0:T(8,128)}), f32[8,16,8,3584]{3,2,1,0:T(8,128)}, u32[]{:S(2)}, u32[]{:S(2)}) %all-to-all-start.6) | async-done | bytes 14680096 | tf_op jit(solution)/shard_map/all_to_all | solution.py:139
  866.5 198.6 %all-to-all-start.9 = ((f32[8,16,8]{2,0,1:T(8,128)}), f32[8,16,8]{2,0,1:T(8,128)S(1)}, u32[]{:S(2)}, u32[]{:S(2)}) async-start(f32[8,16,8]{2,0,1:T(8,128)} %copy.95), calls=%async_computation.9 | async-start | bytes 131072 | tf_op jit(solution)/shard_map/all_to_all | solution.py:147
  1065.1 11.8 copy.92
  1076.9 7.8 all-to-all-start.7
  1084.8 2.3 gather_fusion.7
  1087.8 247.7 %all-to-all-done.7 = f32[8,16,8,3584]{3,2,0,1:T(8,128)} async-done(((f32[8,16,8,3584]{3,2,0,1:T(8,128)}), f32[8,16,8,3584]{3,2,0,1:T(8,128)}, u32[]{:S(2)}, u32[]{:S(2)}) %all-to-all-start.7) | async-done | bytes 14680096 | tf_op jit(solution)/shard_map/all_to_all | solution.py:138
  1335.5 11.8 copy.93
  1347.3 13.3 gather_fusion.6
  1360.6 8.8 reshape.176
  1369.5 8.5 reduce_sum.41
  (98 shorter events, 28.4 us)
Async XLA Ops:
  3.2 2.5 copy-start.2
  24.0 16.8 %all-to-all-start.1 = ((bf16[8,16,8]{2,0,1:T(8,128)(2,1)}), bf16[8,16,8]{2,0,1:T(8,128)(2,1)S(1)}, u32[]{:S(2)}, u32[]{:S(2)}) async-start(bf16[8,16,8]{2,0,1:T(8,128)(2,1)} %copy.83), calls=%async_computation.1 | async-start | bytes 65536 | tf_op jit(solution)/shard_map/all_to_all | solution.py:120
  40.8 5.0 copy-start.1
  40.8 88.4 %all-to-all-start.2 = ((bf16[8,16,8,3584]{3,2,1,0:T(8,128)(2,1)}), bf16[8,16,8,3584]{3,2,1,0:T(8,128)(2,1)}, u32[]{:S(2)}, u32[]{:S(2)}) async-start(bf16[8,16,8,3584]{3,2,1,0:T(8,128)(2,1)} %bitcast.56), calls=%async_computation.2 | async-start | bytes 14680064 | tf_op jit(solution)/shard_map/all_to_all | solution.py:114
  129.2 88.2 %all-to-all-start.4 = ((bf16[8,16,8,3584]{3,2,1,0:T(8,128)(2,1)}), bf16[8,16,8,3584]{3,2,1,0:T(8,128)(2,1)}, u32[]{:S(2)}, u32[]{:S(2)}) async-start(bf16[8,16,8,3584]{3,2,1,0:T(8,128)(2,1)} %bitcast.57), calls=%async_computation.4 | async-start | bytes 14680064 | tf_op jit(solution)/shard_map/all_to_all | solution.py:107
  217.4 130.7 %all-to-all-start.3 = ((bf16[8,16,8,3584]{3,2,0,1:T(8,128)(2,1)}), bf16[8,16,8,3584]{3,2,0,1:T(8,128)(2,1)}, u32[]{:S(2)}, u32[]{:S(2)}) async-start(bf16[8,16,8,3584]{3,2,0,1:T(8,128)(2,1)} %copy.88), calls=%async_computation.3 | async-start | bytes 14680064 | tf_op jit(solution)/shard_map/all_to_all | solution.py:113
  348.1 100.9 %all-to-all-start.5 = ((bf16[8,16,8,3584]{3,2,0,1:T(8,128)(2,1)}), bf16[8,16,8,3584]{3,2,0,1:T(8,128)(2,1)}, u32[]{:S(2)}, u32[]{:S(2)}) async-start(bf16[8,16,8,3584]{3,2,0,1:T(8,128)(2,1)} %copy.90), calls=%async_computation.5 | async-start | bytes 14680064 | tf_op jit(solution)/shard_map/all_to_all | solution.py:106
  479.4 5.2 copy-start
  529.5 5.2 copy-start
  579.6 5.2 copy-start
  629.8 5.2 copy-start
  674.7 24.2 %all-to-all-start.8 = ((f32[8,1,128]{2,1,0:T(1,128)}), f32[8,1,128]{2,1,0:T(1,128)S(1)}, u32[]{:S(2)}, u32[]{:S(2)}) async-start(f32[8,1,128]{2,1,0:T(1,128)} %reshape.290), calls=%async_computation.8 | async-start | bytes 8192 | tf_op jit(solution)/shard_map/all_to_all | solution.py:148
  698.9 167.6 %all-to-all-start.6 = ((f32[8,16,8,3584]{3,2,1,0:T(8,128)}), f32[8,16,8,3584]{3,2,1,0:T(8,128)}, u32[]{:S(2)}, u32[]{:S(2)}) async-start(f32[8,16,8,3584]{3,2,1,0:T(8,128)} %bitcast.55), calls=%async_computation.6 | async-start | bytes 29360128 | tf_op jit(solution)/shard_map/all_to_all | solution.py:139
  866.5 210.3 %all-to-all-start.9 = ((f32[8,16,8]{2,0,1:T(8,128)}), f32[8,16,8]{2,0,1:T(8,128)S(1)}, u32[]{:S(2)}, u32[]{:S(2)}) async-start(f32[8,16,8]{2,0,1:T(8,128)} %copy.95), calls=%async_computation.9 | async-start | bytes 131072 | tf_op jit(solution)/shard_map/all_to_all | solution.py:147
  1076.8 7.8 copy-start.3
  1076.9 258.7 %all-to-all-start.7 = ((f32[8,16,8,3584]{3,2,0,1:T(8,128)}), f32[8,16,8,3584]{3,2,0,1:T(8,128)}, u32[]{:S(2)}, u32[]{:S(2)}) async-start(f32[8,16,8,3584]{3,2,0,1:T(8,128)} %copy.92), calls=%async_computation.7 | async-start | bytes 29360128 | tf_op jit(solution)/shard_map/all_to_all | solution.py:138
where the time goes:
time: 1400 us; the launch traced here: 1380 us
  waiting for transfers between devices  754 us (54%)
  starting transfers between devices  259 us (18%)
  local copies, waits for them, and re-layouts  239 us (17%)
  matrix products  91.2 us (7%)
    all_to_all x1, waiting for transfers between devices, local(): lax.all_to_all(lax.all_to_all(grads.reshape(grid_shape), 'grp', split_axi...  248 us
    all_to_all x1, starting transfers between devices, local(): lax.all_to_all(lax.all_to_all(routes.reshape(grid_shape[:3]), 'grp', spli...  199 us
    all_to_all x1, waiting for transfers between devices, local(): lax.all_to_all(grads.reshape(grid_shape), 'grp', split_axis=0, concat_axi...  160 us
    all_to_all x1, waiting for transfers between devices, local(): lax.all_to_all(lax.all_to_all(sent[1], 'grp', split_axis=0, concat_axis=0...  117 us
    all_to_all x1, waiting for transfers between devices, local(): lax.all_to_all(lax.all_to_all(sent[0], 'grp', split_axis=0, concat_axis=0...  77.4 us
    all_to_all x1, waiting for transfers between devices, local(): lax.all_to_all(sent[0], 'grp', split_axis=0, concat_axis=0, tiled=True)  76.5 us
    all_to_all x1, waiting for transfers between devices, local(): lax.all_to_all(sent[1], 'grp', split_axis=0, concat_axis=0, tiled=True)  76 us
    scatter x8, local copies, waits for them, and re-layouts, one_tile(): return (grads.at[picked].set(contrib), routes.at[picked].set(route_part))  52 us
  transfers between devices with their start and end apart: 9, of which 6 were waited for; matrix products, arithmetic and copies ran while one was open for 5% of the time, Pallas kernels for 0%

commit v1 on v0

v1 whole, which is shorter than its diff:
```python
import jax
import jax.numpy as jnp
from jax import lax
from jax.sharding import PartitionSpec as P

BOTH = ("grp", "ingrp")


def matmul(left, right, kind=jnp.bfloat16):
    return jnp.dot(left, right, preferred_element_type=jnp.float32).astype(kind)


def matmul_t(left, right):
    return lax.dot_general(
        left, right, (((1,), (1,)), ((), ())), preferred_element_type=jnp.float32
    )


def exchange(rows, experts):
    parts = rows.reshape((experts, -1) + rows.shape[1:])
    return lax.all_to_all(parts, BOTH, split_axis=0, concat_axis=0, tiled=True).reshape(rows.shape)


def local(tokens, out_grad, route_weights, expert_ids, w_gate, w_up, w_down):
    tok_rows, width = tokens.shape
    top = expert_ids.shape[1]
    experts = lax.axis_size("grp") * lax.axis_size("ingrp")
    capacity = 2 * tok_rows * top // experts
    slot_total = experts * capacity
    pair_total = tok_rows * top
    gate_mat, up_mat, down_mat = w_gate[0], w_up[0], w_down[0]

    pair_ids = expert_ids.reshape(-1)
    onehot = pair_ids[:, None] == jnp.arange(experts, dtype=jnp.int32)[None, :]
    earlier = (
        jnp.arange(pair_total, dtype=jnp.int32)[:, None]
        > jnp.arange(pair_total, dtype=jnp.int32)[None, :]
    )
    before = matmul(earlier.astype(jnp.bfloat16), onehot.astype(jnp.bfloat16), jnp.float32)
    ranks = jnp.sum(jnp.where(onehot, before, 0.0), axis=1).astype(jnp.int32)
    slots = (pair_ids * capacity + ranks).reshape(tok_rows, top)

    slot_iota = jnp.arange(slot_total, dtype=jnp.int32)
    taken = slots[:, :, None] == slot_iota[None, None, :]
    pick = jnp.any(taken, axis=1).astype(jnp.bfloat16)
    spread = lambda rows: lax.dot_general(
        pick, rows, (((0,), (0,)), ((), ())), preferred_element_type=jnp.float32
    ).astype(jnp.bfloat16)

    rows_x = exchange(spread(tokens), experts)
    rows_dy = exchange(spread(out_grad), experts)

    gate = matmul(rows_x, gate_mat, jnp.float32)
    upper = matmul(rows_x, up_mat, jnp.float32)
    sigma = jax.nn.sigmoid(gate)
    active = gate * sigma
    slope = upper * sigma * (1.0 + gate * (1.0 - sigma))
    raw = matmul_t(rows_dy, down_mat)
    route_part = jnp.sum(raw * (active * upper), axis=1)
    d_gate = (raw * slope).astype(jnp.bfloat16)
    d_upper = (raw * active).astype(jnp.bfloat16)
    contrib = (matmul_t(d_gate, gate_mat) + matmul_t(d_upper, up_mat)).astype(jnp.bfloat16)

    back_routes = exchange(route_part, experts)
    back = exchange(contrib, experts)

    weights = jnp.sum(
        jnp.where(taken, route_weights[:, :, None], jnp.zeros((), jnp.bfloat16)), axis=1
    )
    x_grad = matmul(weights, back)
    route_grad = jnp.sum(jnp.where(taken, back_routes[None, None, :], 0.0), axis=2)
    return (x_grad, route_grad)


def solution(mesh):
    return jax.shard_map(
        local,
        mesh=mesh,
        in_specs=(
            P(BOTH, None),
            P(BOTH, None),
            P(BOTH, None),
            P(BOTH, None),
            P(BOTH, None, None),
            P(BOTH, None, None),
            P(BOTH, None, None),
        ),
        out_specs=(P(BOTH, None), P(BOTH, None)),
        check_vma=False,
    )
```

time: 1400 us -> 369 us (0.26); the launches traced: 1380 us -> 369 us
  waiting for transfers between devices: 754 us -> 235 us
  local copies, waits for them, and re-layouts: 239 us -> 2.49 us
  starting transfers between devices: 259 us -> 32.2 us
    all_to_all x9 -> x4, waiting for transfers between devices: 754 us -> 235 us  [exchange(): lax.all_to_all(parts, BOTH, split_axis=0, concat_axis=0, tiled=True)]
    all_to_all x9 -> x4, starting transfers between devices: 259 us -> 32.2 us  [exchange(): lax.all_to_all(parts, BOTH, split_axis=0, concat_axis=0, tiled=True)]
    gather x17 -> x0, local copies, waits for them, and re-layouts: 90.7 us -> none  [the longest x4 24.3 us: one_tile(): dy_padded[picked]]
    scatter x10 -> x0, local copies, waits for them, and re-layouts: 58.7 us -> none  [the longest x8 52 us: one_tile(): return (grads.at[picked].set(contrib), routes.at[picked].set(route_part))]
    all_to_all x12 -> x2, local copies, waits for them, and re-layouts: 46.8 us -> 1.23 us  [exchange(): lax.all_to_all(parts, BOTH, split_axis=0, concat_axis=0, tiled=True)]
    dot_general x20 -> x9, matrix products: 91.2 us -> 95.3 us  [the longest x3 52.3 us: matmul_t(): lax.dot_general(left, right, (((1,), (1,)), ((), ())), preferred_element_...]
  transfers between devices with their start and end apart: 9 -> 4, of which waited for: 6 -> 3; matrix products, arithmetic and copies ran while one was open for 5% -> 14% of each run, Pallas kernels for 0% -> 0%
where the time goes in v1:
time: 369 us
  waiting for transfers between devices  235 us (64%)
  matrix products  95.3 us (26%)
  starting transfers between devices  32.2 us (9%)
    all_to_all x4, waiting for transfers between devices, exchange(): lax.all_to_all(parts, BOTH, split_axis=0, concat_axis=0, tiled=True)  235 us
    dot_general x3, matrix products, matmul_t(): lax.dot_general(left, right, (((1,), (1,)), ((), ())), preferred_element_...  52.3 us
    dot_general x4, matrix products, matmul(): return jnp.dot(left, right, preferred_element_type=jnp.float32).astype(kind)  32.8 us
    all_to_all x4, starting transfers between devices, exchange(): lax.all_to_all(parts, BOTH, split_axis=0, concat_axis=0, tiled=True)  32.2 us
    dot_general x2, matrix products, local(): lax.dot_general(pick, rows, (((0,), (0,)), ((), ())), preferred_element_t...  10.2 us
  transfers between devices with their start and end apart: 4, of which 3 were waited for; matrix products, arithmetic and copies ran while one was open for 14% of the time, Pallas kernels for 0%

profile of v1, /device:TPU:6, one launch (start us, length us, event | category | flops | bytes accessed | tf_op | source)
XLA Modules:
  0.0 368.8 jit_solution(7189019019928017266)
XLA Ops:
  0.6 0.0 copy-start
  0.6 0.9 copy.25
  1.5 0.1 eq.28
  1.6 0.3 fusion.26
  2.0 0.1 convert_element_type.32
  2.1 0.1 copy.26
  2.1 0.7 multiply_add_fusion
  2.8 0.4 fusion.24
  3.2 0.0 copy-done
  3.2 5.1 %fusion.15 = bf16[128,8,3584]{2,1,0:T(8,128)(2,1)} fusion(pred[128,1024]{1,0:T(8,128)(4,1)S(1)} %fusion.24, bf16[128,3584]{1,0:T(8,128)(2,1)S(1)} %copy-done), kind=kOutput, calls=%fused_computation.18 | convolution fusion | flops 943194112 | bytes 8388608 | tf_op jit(solution)/shard_map/dot_general | solution.py:46
  8.3 0.0 copy-start.2
  8.3 10.9 %all-to-all-start.1 = ((bf16[128,8,3584]{2,1,0:T(8,128)(2,1)}), bf16[128,8,3584]{2,1,0:T(8,128)(2,1)}, u32[]{:S(2)}, u32[]{:S(2)}) async-start(bf16[128,8,3584]{2,1,0:T(8,128)(2,1)} %fusion.15), calls=%async_computation.1 | async-start | bytes 14680064 | tf_op jit(solution)/shard_map/all_to_all | solution.py:21
  19.2 0.0 copy-done.2
  19.2 5.1 %fusion.14 = bf16[128,8,3584]{2,1,0:T(8,128)(2,1)} fusion(pred[128,1024]{1,0:T(8,128)(4,1)S(1)} %fusion.24, bf16[128,3584]{1,0:T(8,128)(2,1)S(1)} %copy-done.2), kind=kOutput, calls=%fused_computation.17 | convolution fusion | flops 943194112 | bytes 8388608 | tf_op jit(solution)/shard_map/dot_general | solution.py:46
  24.4 84.9 %all-to-all-done.1 = bf16[128,8,3584]{2,1,0:T(8,128)(2,1)} async-done(((bf16[128,8,3584]{2,1,0:T(8,128)(2,1)}), bf16[128,8,3584]{2,1,0:T(8,128)(2,1)}, u32[]{:S(2)}, u32[]{:S(2)}) %all-to-all-start.1) | async-done | bytes 7340064 | tf_op jit(solution)/shard_map/all_to_all | solution.py:21
  109.2 5.8 %all-to-all-start = ((bf16[128,8,3584]{2,1,0:T(8,128)(2,1)}), bf16[128,8,3584]{2,1,0:T(8,128)(2,1)}, u32[]{:S(2)}, u32[]{:S(2)}) async-start(bf16[128,8,3584]{2,1,0:T(8,128)(2,1)} %fusion.14), calls=%async_computation | async-start | bytes 14680064 | tf_op jit(solution)/shard_map/all_to_all | solution.py:21
  115.0 13.7 %fusion.4 = f32[1024,1024]{0,1:T(8,128)} fusion(bf16[1,3584,1024]{2,1,0:T(8,128)(2,1)} %param.11, bf16[128,8,3584]{2,1,0:T(8,128)(2,1)} %all-to-all-done.1), kind=kOutput, calls=%fused_computation.7 | convolution fusion | flops 7516192768 | bytes 18874368 | tf_op jit(solution)/shard_map/dot_general | solution.py:10
  128.7 13.7 %fusion.7 = f32[1024,1024]{0,1:T(8,128)} fusion(bf16[1,3584,1024]{2,1,0:T(8,128)(2,1)} %param.12, bf16[128,8,3584]{2,1,0:T(8,128)(2,1)} %all-to-all-done.1), kind=kOutput, calls=%fused_computation.10 | convolution fusion | flops 7516192768 | bytes 18874368 | tf_op jit(solution)/shard_map/dot_general | solution.py:10
  142.4 62.7 %all-to-all-done = bf16[128,8,3584]{2,1,0:T(8,128)(2,1)} async-done(((bf16[128,8,3584]{2,1,0:T(8,128)(2,1)}), bf16[128,8,3584]{2,1,0:T(8,128)(2,1)}, u32[]{:S(2)}, u32[]{:S(2)}) %all-to-all-start) | async-done | bytes 7340064 | tf_op jit(solution)/shard_map/all_to_all | solution.py:21
  205.1 0.0 copy-start.4
  205.1 14.6 %multiply_reduce_fusion = (f32[1024]{0:T(1024)S(1)}, f32[1024,1024]{0,1:T(8,128)S(1)}) fusion(f32[1024,1024]{0,1:T(8,128)} %fusion.7, f32[1024,1024]{0,1:T(8,128)} %fusion.4, bf16[1,1024,3584]{2,1,0:T(8,128)(2,1)} %param.13, bf16[128,8,3584]{2,1,0:T(8,128)(2,1)} %all-to-all-done), kind=kOutput, calls=%fused_computation.21 | convolution fusion | flops 7523531776 | bytes 27267072 | tf_op jit(solution)/shard_map/dot_general | solution.py:14
  219.6 0.0 copy-start.5
  219.6 0.0 copy-done.4
  219.6 19.4 %fusion.2 = f32[1024,3584]{1,0:T(8,128)} fusion(bf16[1,3584,1024]{2,1,0:T(8,128)(2,1)} %param.11, f32[1024,1024]{0,1:T(8,128)S(1)} %get-tuple-element.3, f32[1024,1024]{0,1:T(8,128)S(1)} %copy-done.4, f32[1024,1024]{0,1:T(8,128)} %fusion.7), kind=kOutput, calls=%fused_computation.5 | convolution fusion | flops 7526678528 | bytes 34603008 | tf_op jit(solution)/shard_map/dot_general | solution.py:14
  239.0 0.0 copy-done.5
  239.0 0.7 all_to_all.18
  239.8 5.4 %all-to-all-start.3 = ((f32[128,1,8]{2,1,0:T(1,128)}), f32[128,1,8]{2,1,0:T(1,128)S(1)}, u32[]{:S(2)}, u32[]{:S(2)}) async-start(f32[128,1,8]{2,1,0:T(1,128)} %bitcast.9), calls=%async_computation.3 | async-start | bytes 131072 | tf_op jit(solution)/shard_map/all_to_all | solution.py:21
  245.1 18.3 %fusion.16 = bf16[128,8,3584]{2,1,0:T(8,128)(2,1)} fusion(f32[1024,3584]{1,0:T(8,128)} %fusion.2, bf16[1,3584,1024]{2,1,0:T(8,128)(2,1)} %param.12, f32[1024,1024]{0,1:T(8,128)} %copy-done.5, f32[1024,1024]{0,1:T(8,128)} %fusion.4), kind=kOutput, calls=%fused_computation.19 | convolution fusion | flops 7529824256 | bytes 37748736 | tf_op jit(solution)/shard_map/dot_general | solution.py:14
  263.5 0.0 copy-start.3
  263.5 0.0 all-to-all-done.3
  263.5 10.2 %all-to-all-start.2 = ((bf16[128,8,3584]{2,1,0:T(8,128)(2,1)}), bf16[128,8,3584]{2,1,0:T(8,128)(2,1)}, u32[]{:S(2)}, u32[]{:S(2)}) async-start(bf16[128,8,3584]{2,1,0:T(8,128)(2,1)} %fusion.16), calls=%async_computation.2 | async-start | bytes 14680064 | tf_op jit(solution)/shard_map/all_to_all | solution.py:21
  273.6 0.0 copy-done.3
  273.7 0.3 fusion.27
  274.0 0.5 broadcast.21
  274.5 0.8 reduce.4
  275.3 0.1 broadcast_in_dim.38
  275.4 0.0 copy-start.1
  275.4 0.9 select_reduce_fusion
  276.3 87.3 %all-to-all-done.2 = bf16[128,8,3584]{2,1,0:T(8,128)(2,1)} async-done(((bf16[128,8,3584]{2,1,0:T(8,128)(2,1)}), bf16[128,8,3584]{2,1,0:T(8,128)(2,1)}, u32[]{:S(2)}, u32[]{:S(2)}) %all-to-all-start.2) | async-done | bytes 7340064 | tf_op jit(solution)/shard_map/all_to_all | solution.py:21
  363.6 5.2 %fusion.19 = bf16[128,3584]{1,0:T(8,128)(2,1)} fusion(bf16[128,1024]{1,0:T(8,128)(2,1)S(1)} %fusion.27, bf16[128,8,3584]{2,1,0:T(8,128)(2,1)} %all-to-all-done.2), kind=kOutput, calls=%fused_computation.20 | convolution fusion | flops 939982848 | bytes 8519680 | tf_op jit(solution)/shard_map/dot_general | solution.py:10
  368.8 0.0 copy-done.1
  (1 shorter events, 0.0 us)
Async XLA Ops:
  0.6 2.6 copy-start
  8.3 10.9 %copy-start.2 = (bf16[128,3584]{1,0:T(8,128)(2,1)S(1)}, bf16[128,3584]{1,0:T(8,128)(2,1)}, u32[]{:S(2)}) copy-start(bf16[128,3584]{1,0:T(8,128)(2,1)} %param.8) | copy-start | bytes 2752516
  8.3 100.9 %all-to-all-start.1 = ((bf16[128,8,3584]{2,1,0:T(8,128)(2,1)}), bf16[128,8,3584]{2,1,0:T(8,128)(2,1)}, u32[]{:S(2)}, u32[]{:S(2)}) async-start(bf16[128,8,3584]{2,1,0:T(8,128)(2,1)} %fusion.15), calls=%async_computation.1 | async-start | bytes 14680064 | tf_op jit(solution)/shard_map/all_to_all | solution.py:21
  109.2 95.8 %all-to-all-start = ((bf16[128,8,3584]{2,1,0:T(8,128)(2,1)}), bf16[128,8,3584]{2,1,0:T(8,128)(2,1)}, u32[]{:S(2)}, u32[]{:S(2)}) async-start(bf16[128,8,3584]{2,1,0:T(8,128)(2,1)} %fusion.14), calls=%async_computation | async-start | bytes 14680064 | tf_op jit(solution)/shard_map/all_to_all | solution.py:21
  205.1 14.6 %copy-start.4 = (f32[1024,1024]{0,1:T(8,128)S(1)}, f32[1024,1024]{0,1:T(8,128)}, u32[]{:S(2)}) copy-start(f32[1024,1024]{0,1:T(8,128)} %fusion.4) | copy-start | bytes 12582916
  219.6 19.4 %copy-start.5 = (f32[1024,1024]{0,1:T(8,128)}, f32[1024,1024]{0,1:T(8,128)S(1)}, u32[]{:S(2)}) copy-start(f32[1024,1024]{0,1:T(8,128)S(1)} %get-tuple-element.3) | copy-start | bytes 12582916
  239.8 23.7 %all-to-all-start.3 = ((f32[128,1,8]{2,1,0:T(1,128)}), f32[128,1,8]{2,1,0:T(1,128)S(1)}, u32[]{:S(2)}, u32[]{:S(2)}) async-start(f32[128,1,8]{2,1,0:T(1,128)} %bitcast.9), calls=%async_computation.3 | async-start | bytes 131072 | tf_op jit(solution)/shard_map/all_to_all | solution.py:21
  263.5 10.2 %copy-start.3 = (bf16[128,4]{0,1:T(4,128)(2,1)S(1)}, bf16[128,4]{0,1:T(4,128)(2,1)}, u32[]{:S(2)}) copy-start(bf16[128,4]{0,1:T(4,128)(2,1)} %param.9) | copy-start | bytes 3076
  263.5 100.2 %all-to-all-start.2 = ((bf16[128,8,3584]{2,1,0:T(8,128)(2,1)}), bf16[128,8,3584]{2,1,0:T(8,128)(2,1)}, u32[]{:S(2)}, u32[]{:S(2)}) async-start(bf16[128,8,3584]{2,1,0:T(8,128)(2,1)} %fusion.16), calls=%async_computation.2 | async-start | bytes 14680064 | tf_op jit(solution)/shard_map/all_to_all | solution.py:21
  275.4 93.4 %copy-start.1 = (bf16[128,3584]{1,0:T(8,128)(2,1)S(1)}, bf16[128,3584]{1,0:T(8,128)(2,1)}, u32[]{:S(2)}) copy-start(bf16[128,3584]{1,0:T(8,128)(2,1)} %param.7) | copy-start | bytes 2752516
